TPU v7x, 256 devices: a whole 4x4x8 slice. The times are simulated.
256 devices in a mesh: clus: 16 (over x_lo, z), blk: 16 (over x_hi, y, core).
Axes of the slice: x: 4 (x_hi: 2, x_lo: 2; x = x_hi * 2 + x_lo), y: 4, z: 8, core: 2. Of those that a mesh axis runs over, the one named last changes fastest.
Arguments:
- embeddings: bfloat16 [163840, 1024], P(('clus', 'blk')), parts along dimension 0, as said below
- cluster_ids: int32 [163840], P(('clus', 'blk')), parts along dimension 0, may hold values from 0 to 7, never falling along the last dimension, each value on 1 to 5120 neighbouring positions
- valid: int32 [163840], P(('clus', 'blk')), parts along dimension 0, may hold values 0 or 1
Outputs:
- nearest: float32 [163840], P(('clus', 'blk')), parts along dimension 0
There are 16 independent parts, one for each index of `clus`. A program takes and returns all parts, laid end to end along the dimension named above; each array names one. Nothing has to cross between parts.
Inputs may be any that keep to these rules, and one draw needn't show every extreme that they name: Each row of embeddings is finite and not all zero.
All inputs are finite; a program needn't handle non-finite values. No bound on the sum of `valid` on one device may be relied on, other than what follows from the above.
Results may differ from a plain program's by a relative error of at most 0.00039.
Values may be sent and summed in bfloat16 or wider, within the bound.
No kernel may reach another device: no remote copies, remote signals or barrier semaphores. Data moves between devices by JAX's collectives and lax.ppermute only.
A program may use at most 64 MiB of HBM per device.

v0:
```python
import jax
import jax.numpy as jnp
from jax import lax
from jax.sharding import PartitionSpec as P


def normalize(embeddings):
    values = embeddings.astype(jnp.float32)
    scale = lax.rsqrt(jnp.sum(values * values, axis=1) + 1e-06)
    return (values * scale[:, None]).astype(jnp.bfloat16)


def masked_tile(query, q_label, q_pos, keys, k_label, k_pos):
    scores = jnp.dot(query, keys.T, preferred_element_type=jnp.float32)
    match = (
        (q_label[:, None] == k_label[None, :])
        & (q_label[:, None] >= 0)
        & (q_pos[:, None] != k_pos[None, :])
    )
    return jnp.where(match, scores, -1.0)


def shards(embeddings, cluster_ids, valid):
    own = lax.axis_index("blk")
    rows = embeddings.shape[0]
    unit = normalize(embeddings)
    label = jnp.where(valid > 0, cluster_ids, -1)
    all_labels = lax.all_gather(label, "blk", axis=0, tiled=True)
    own_pos = own * rows + jnp.arange(rows, dtype=jnp.int32)
    piece = lax.all_gather(unit, "blk", axis=0, tiled=True)
    width = piece.shape[0]
    k_pos = jnp.arange(width, dtype=jnp.int32)
    tile = masked_tile(unit, label, own_pos, piece, all_labels, k_pos)
    return jnp.maximum(jnp.full((rows,), -1.0, jnp.float32), jnp.max(tile, axis=1))


def solution(mesh):
    return jax.shard_map(
        shards,
        mesh=mesh,
        in_specs=(P(("clus", "blk"), None), P(("clus", "blk")), P(("clus", "blk"))),
        out_specs=P(("clus", "blk")),
        check_vma=False,
    )
```

profile of v0, /device:TPU:1, one launch (start us, length us, event | category | flops | bytes accessed | tf_op | source)
XLA Modules:
  0.0 178.1 jit_solution(7722314262681008759)
XLA Ops:
  6.5 0.0 all-gather.3.cloned.1.call-start
  6.5 1.6 fusion.1
  8.2 2.7 %fusion.2 = bf16[640,1024]{1,0:T(8,128)(2,1)} fusion(bf16[640,1024]{1,0:T(8,128)(2,1)} %param.3, f32[640]{0:T(1024)S(1)} %add_rsqrt_fusion), kind=kLoop, calls=%fused_computation.6 | loop fusion | flops 1966080 | bytes 2624000 | tf_op jit(solution)/shard_map/convert_element_type | solution.py:10
  10.8 0.0 all-gather.3.cloned.1.call-update
  10.9 0.7 broadcast_compare_fusion
  11.6 25.9 %all-gather = s32[16,1,640]{2,1,0:T(1,128)S(1)} all-gather(s32[1,1,640]{2,1,0:T(1,128)S(1)} %reshape.12), channel_id=1, replica_groups=mesh['clus'=16,'blk'=16] {'blk'}, dimensions={0}, use_global_device_ids=true | all-gather | bytes 43520 | tf_op jit(solution)/shard_map/all_gather | solution.py:28
  37.5 111.2 %all-gather.3.cloned.1.call-done = bf16[10240,1024]{1,0:T(8,128)(2,1)} async-done(((bf16[640,1024]{1,0:T(8,128)(2,1)}), bf16[10240,1024]{1,0:T(8,128)(2,1)}) %all-gather.3.cloned.1.call-update) | async-done | bytes 20971536 | tf_op jit(solution)/shard_map/all_gather | solution.py:30
  148.7 21.9 %select_reduce_fusion = f32[640]{0:T(1024)S(1)} fusion(bf16[640,1024]{1,0:T(8,128)(2,1)} %fusion.2, bf16[10240,1024]{1,0:T(8,128)(2,1)} %all-gather.3.cloned.1.call-done, s32[640]{0:T(1024)S(1)} %iota_add_fusion, s32[10240]{0:T(1024)S(1)} %bitcast.3, s32[640]{0:T(1024)S(1)} %get-tuple-element.6, pred[640]{0:T(1024)(128)(4,1)S(1)} %get-tuple-element.5), kind=kOutput, calls=%fused_computation | convolution fusion | flops 13461093376 | bytes 22331520 | tf_op jit(solution)/shard_map/dot_general | solution.py:14
  170.7 0.6 broadcast_maximum_fusion
  (3 shorter events, 0.0 us)
Async XLA Ops:
  6.5 142.2 %all-gather.3.cloned.1.call-start = ((), (), s32[]{:S(2)}) async-start(), calls=%async_computation | async-start | bytes 22282240 | tf_op jit(solution)/shard_map/all_gather | solution.py:30
Sparse Core Ops, SparseCore 0:
  11.0 137.6 all-gather.2
where the time goes:
time: 178 us
  waiting for transfers between devices  111 us (62%)
  blocking collectives  25.9 us (15%)
  matrix products  21.9 us (12%)
  between operations  13.4 us (8%)
  other arithmetic  5.62 us (3%)
    all_gather x1, waiting for transfers between devices, shards(): piece = lax.all_gather(unit, 'blk', axis=0, tiled=True)  111 us
    all_gather x1, blocking collectives, shards(): all_labels = lax.all_gather(label, 'blk', axis=0, tiled=True)  25.9 us
    dot_general x1, matrix products, masked_tile(): scores = jnp.dot(query, keys.T, preferred_element_type=jnp.float32)  21.9 us
  transfers between devices with their start and end apart: 1, of which 1 were waited for; matrix products, arithmetic and copies ran while one was open for 0% of the time, Pallas kernels for 0%

commit v1 on v0

v1 whole, which is shorter than its diff:
```python
import functools

import jax
import jax.numpy as jnp
import numpy as np
from jax import lax
from jax.experimental import pallas as pl
from jax.experimental.pallas import tpu as pltpu
from jax.sharding import PartitionSpec as P

N = 16
PAD = 16

MODE = (1, 0, 0, 0, 2, 3, 1, 2)


def up(chip):
    return chip // 4 * 4 + (chip + 1) % 4


def down(chip):
    return chip // 4 * 4 + (chip + 3) % 4


ALONG = [(2 * c, 2 * up(c)) for c in range(8)] + [(2 * c + 1, 2 * down(c) + 1) for c in range(8)]
PASSES_ON = [MODE[d // 2] >> d % 2 & 1 for d in range(N)]
BUDDY = [(d, d ^ 1) for d in range(N)]
ACROSS = [(d, d ^ 8) for d in range(N)]


def arrived(held, moves):
    got = [-1] * N
    for s, t in moves:
        got[t] = held[s]
    return got


OF = [list(range(N))]
OF.append(arrived(OF[0], BUDDY))
OF.append(arrived(OF[0], ALONG))
OF.append(arrived(OF[2], BUDDY))
OF.append(arrived(OF[0], ACROSS))
OF.append(arrived(OF[4], BUDDY))
OF.append(arrived([OF[2 if PASSES_ON[d] else 1][d] for d in range(N)], ALONG))
LATE = (6, 7)

WORK = (
    [[[(0, 1), (0, 6), (3, 6)], [(1, 8), (6, 8)], [(3, 7), (7, 8)]],
     [[(1, 3)], [(1, 9), (3, 9)], [(1, 2), (2, 9)]],
     [[(0, 2), (2, 3)], [], [(2, 6), (6, 10)]],
     [[(0, 3), (0, 5), (3, 5)], [(3, 11), (5, 11)], [(0, 4), (4, 11)]],
     [[(2, 4), (2, 5), (4, 5)], [(5, 12)], [(3, 4)]],
     [[(2, 7), (5, 7)], [(5, 13), (7, 13)], [(6, 13)]],
     [[(1, 6), (4, 6), (6, 7)], [(6, 14), (7, 14)], [(1, 5), (5, 6)]],
     [[(1, 4), (1, 7), (4, 7)], [(7, 15)], [(0, 7)]],
     [[(8, 11), (8, 14), (11, 14)], [(0, 8)], [(8, 15), (11, 15)]],
     [[(8, 9), (9, 11), (9, 14)], [], [(9, 13), (13, 14)]],
     [[(8, 10)], [(2, 8), (2, 10)], [(9, 10)]],
     [[(8, 13), (10, 11), (11, 13)], [(3, 8), (3, 10)], [(8, 12), (11, 12)]],
     [[(10, 12), (12, 13)], [(4, 10), (4, 12)], [(4, 8), (5, 8)]],
     [[(10, 13), (10, 15), (13, 15)], [(5, 10)], [(4, 9), (5, 9)]],
     [[(9, 12), (12, 14), (14, 15)], [(6, 9), (6, 12)], [(7, 10), (10, 14)]],
     [[(9, 15), (12, 15), (14, 15)], [(7, 9), (7, 12)], [(6, 11), (7, 11)]]])

BACK = (
    (),
    (
        (1, -1, 0, -1, 5, 2, 7, 4, -1, 11, 8, 3, 13, 10, 6, 9),
        (6, -1, 3, 5, -1, 7, 4, -1, 0, 8, -1, 13, 10, 15, 9, 12),
    ),
    (
        (3, 9, 10, 0, 12, -1, 14, 1, 11, 13, 2, 8, 5, 4, 7, 6),
        (8, 2, 6, 11, 3, 13, 1, 0, 15, 14, 9, 10, 4, 5, 12, 7),
        (7, 3, -1, 4, 2, 6, 5, 15, 14, -1, -1, 12, 8, 9, 10, 11),
    ),
)


def check():
    served = set()
    for d in range(N):
        for stage, pairs in enumerate(WORK[d]):
            for a, b in pairs:
                for owner, partner in ((a, b), (b, a)):
                    if owner == d or any(row[d] == owner for later in BACK[stage:] for row in later):
                        served.add((owner, partner))
    assert all((a, b) in served for a in range(N) for b in range(N) if 0 < abs(a - b) <= 8)


check()


def full(row):
    free = [t for t in range(N) if t not in row]
    return [(d, t if t >= 0 else free.pop()) for d, t in enumerate(row)]


def grouped(pairs, lead):
    left, order = list(pairs), []
    while left:
        if not any(lead in p for p in left):
            lead = max(range(N), key=lambda b: sum(b in p for p in left))
        group = [p for p in left if lead in p]
        order += [(lead, p[0] + p[1] - lead) for p in group]
        left = [p for p in left if lead not in p]
    return order


FIELDS = 5
LATER = 6
COST = (0, 2 * 10 ** 10, 0)


def first_schedule():
    longest = max(len(WORK[d][0]) for d in range(N))
    use = np.zeros((N, 4), np.int32)
    pairs = np.full((N, longest * FIELDS), -1, np.int32)
    for d in range(N):
        slot = {OF[s][d]: s for s in reversed(range(4))}
        order = grouped(WORK[d][0], d)
        for k, (a, b) in enumerate(order):
            use[d, slot[a]] |= 1
            use[d, slot[b]] |= 2
            end = k + 1 == len(order) or order[k + 1][0] != a
            pairs[d, FIELDS * k:FIELDS * (k + 1)] = slot[a], slot[b], a, b, end
        use[d, 0] = 3
        for stage, lead in ((1, 4), (2, 6)):
            for pair in WORK[d][stage]:
                for b in pair:
                    if b != OF[lead][d] and b in slot:
                        use[d, slot[b]] |= 2
    return use, pairs


def late_schedule(stage, lead):
    early = np.zeros((N, 2 + 2 * LATER), np.int32)
    other = np.zeros((N, 4), np.int32)
    for d in range(N):
        own = OF[lead][d]
        slot = {OF[s][d]: s for s in reversed(range(lead))}
        partners = [p[0] + p[1] - own for p in WORK[d][stage]]
        assert all(own in p for p in WORK[d][stage])
        near = [b for b in partners if slot[b] < 4]
        early[d, :2] = own, len(near)
        for k, b in enumerate(near):
            early[d, 2 + 2 * k:4 + 2 * k] = slot[b], b
        for b in partners:
            if slot[b] >= 4:
                assert not other[d, slot[b] - 4]
                other[d, slot[b] - 4], other[d, slot[b] - 2] = 1, b
    return early, other


def pack_kernel(ids_in, valid_in, rows_in, out, out_x, ids, valid, raw, unit, in_sems, out_sems):
    rows, depth = raw.shape
    parts = [pl.ds(at, 128) for at in range(0, rows, 128)]
    tail = pl.ds(rows, 2 * PAD)
    loads = [pltpu.make_async_copy(rows_in.at[p], raw.at[p], in_sems.at[k]) for k, p in enumerate(parts)]
    small = [pltpu.make_async_copy(ids_in, ids, in_sems.at[len(parts)]),
             pltpu.make_async_copy(valid_in, valid, in_sems.at[len(parts) + 1])]
    ends = parts + [pl.ds(rows, PAD)], parts + [tail]
    stores = [[pltpu.make_async_copy(unit.at[p], ref.at[p], out_sems.at[n, k]) for n, (ref, p) in enumerate(zip((out, out_x), both))]
              for k, both in enumerate(zip(*ends))]
    for load in loads[:1] + small + loads[1:]:
        load.start()
    for k, (load, part) in enumerate(zip(loads, parts)):
        load.wait()
        values = raw[part, :].astype(jnp.float32)
        scale = lax.rsqrt(jnp.sum(values * values, axis=1, keepdims=True) + 1e-06)
        unit[part, :] = (values * scale).astype(jnp.bfloat16)
        [store.start() for store in stores[k]]
        if k == 0:
            for load in small:
                load.wait()
            label = jnp.where(valid[...] > 0, ids[...], -1).astype(jnp.float32).reshape(1, rows)
            label = jnp.concatenate([label, jnp.zeros((1, depth - rows), jnp.float32)], axis=1)
            unit[tail, :] = jnp.broadcast_to(label, (2 * PAD, depth)).astype(jnp.bfloat16)
            [store.start() for store in stores[-1]]
    for store in sum(stores, []):
        store.wait()


def pack(embeddings, cluster_ids, valid):
    rows, depth = embeddings.shape
    anywhere = pl.BlockSpec(memory_space=pl.ANY)
    return pl.pallas_call(
        pack_kernel,
        out_shape=[jax.ShapeDtypeStruct((rows + n * PAD, depth), jnp.bfloat16) for n in (1, 2)],
        in_specs=[anywhere] * 3,
        out_specs=[anywhere] * 2,
        scratch_shapes=[
            pltpu.VMEM((rows,), jnp.int32),
            pltpu.VMEM((rows,), jnp.int32),
            pltpu.VMEM((rows, depth), jnp.bfloat16),
            pltpu.VMEM((rows + 2 * PAD, depth), jnp.bfloat16),
            pltpu.SemaphoreType.DMA((rows // 128 + 2,)),
            pltpu.SemaphoreType.DMA((2, rows // 128 + 1)),
        ],
        compiler_params=pltpu.CompilerParams(vmem_limit_bytes=58 * 2 ** 20),
        cost_estimate=pl.CostEstimate(flops=4 * rows * depth, bytes_accessed=4 * rows * depth, transcendentals=rows),
    )(cluster_ids, valid, embeddings)


def turn(block, to):
    rows = to.shape[1]

    def part(k, _):
        at = pl.ds(pl.multiple_of(k * 128, 128), 128)
        to[:, at] = jnp.transpose(block[at, :])
        return 0

    lax.fori_loop(0, rows // 128, part, 0)


def row_labels(block, rows):
    label = block[rows:rows + PAD, :rows].astype(jnp.float32)
    return jnp.transpose(jnp.broadcast_to(label[:1], (128, rows)))


def column_labels(block, rows):
    label = block[rows:rows + PAD, :rows].astype(jnp.float32)[:8]
    return jnp.where(label < 0.0, -2.0, label)


def tile(left, right, labels, keys, racc, out, b, own):
    rows, wide, step = racc.shape[0], 256, 64
    for at in range(0, rows, wide):
        lanes = [slice(c, c + 128) for c in range(0, min(wide, rows - at), 128)]
        scores = jnp.dot(left, right[:, at:at + 128 * len(lanes)], preferred_element_type=jnp.float32)
        key = [keys[:, at + c.start:at + c.stop][None] for c in lanes]
        low = [jnp.full((8, 128), -1.0, jnp.float32) for _ in lanes]
        for r in range(0, rows, step):
            label = labels[r:r + step, :].reshape(step // 8, 8, 128)
            high = racc[r:r + step, :].reshape(step // 8, 8, 128)
            for n, c in enumerate(lanes):
                match = label == key[n]
                if own:
                    row = r + 8 * lax.broadcasted_iota(jnp.int32, (step // 8, 8, 128), 0) + (
                        lax.broadcasted_iota(jnp.int32, (step // 8, 8, 128), 1))
                    col = lax.broadcasted_iota(jnp.int32, (step // 8, 8, 128), 2) + (at + c.start)
                    match = match & (row != col)
                part = jnp.where(match, scores[r:r + step, c].reshape(step // 8, 8, 128), -1.0)
                high = jnp.maximum(high, part)
                if not own:
                    low[n] = jnp.maximum(low[n], jnp.max(part, axis=0))
            racc[r:r + step, :] = high.reshape(step, 128)
        if not own:
            for n, c in enumerate(lanes):
                cols = slice(at + c.start, at + c.stop)
                out[b, :, cols] = jnp.maximum(out[b, :, cols], jnp.max(low[n], axis=0, keepdims=True))


def flush(racc, out, a):
    most = jnp.max(jnp.transpose(racc[...]), axis=0, keepdims=True)
    out[a] = jnp.maximum(out[a], most)
    racc[...] = jnp.full_like(racc, -1.0)


def give(out, back, results):
    me = lax.axis_index("blk")
    for k, result in enumerate(results):
        to = back[me, k]
        result[...] = jnp.where(to >= 0, out[jnp.maximum(to, 0)], -1.0)


def first_kernel(count, returns, use, pairs, back, *refs):
    blocks, (out, turned, lkey), results = refs[:4], refs[4:7], refs[7:7 + returns]
    unit, lcol, racc = refs[7 + returns:]
    rows = racc.shape[0]
    me = lax.axis_index("blk")
    out[...] = jnp.full_like(out, -1.0)
    racc[...] = jnp.full_like(racc, -1.0)
    for s, block in enumerate(blocks):
        lkey[s] = column_labels(block, rows)

        @pl.when((use[me, s] & 1) > 0)
        def _(s=s, block=block):
            def fetch(k, _):
                at = pl.ds(pl.multiple_of(k * 128, 128), 128)
                unit[s, at, :] = block[at, :]
                return 0

            lax.fori_loop(0, rows // 128, fetch, 0)
            lcol[s] = row_labels(block, rows)

        @pl.when((use[me, s] & 2) > 0)
        def _(s=s, block=block):
            turn(block, turned.at[s])

    tile(unit[0], turned.at[0], lcol.at[0], lkey.at[0], racc, out, None, True)

    @pl.when(pairs[me, 0] != 0)
    def _():
        flush(racc, out, me)

    def each(k, _):
        i, j, a, b, end = [pairs[me, FIELDS * k + n] for n in range(FIELDS)]

        @pl.when(i >= 0)
        def _():
            tile(unit[i], turned.at[j], lcol.at[i], lkey.at[j], racc, out, b, False)

            @pl.when(end > 0)
            def _():
                flush(racc, out, a)

        return 0

    lax.fori_loop(0, count, each, 0)
    give(out, back, results)


def with_early(me, early, block, turned, lkey, lcol, racc, out):
    rows = racc.shape[0]
    lcol[...] = row_labels(block, rows)
    racc[...] = jnp.full_like(racc, -1.0)

    def each(k, _):
        j, b = early[me, 2 + 2 * k], early[me, 3 + 2 * k]
        tile(block[:rows, :], turned.at[j], lcol, lkey.at[j], racc, out, b, False)
        return 0

    lax.fori_loop(0, early[me, 1], each, 0)


def second_kernel(returns, early, meets, back, far, turned, lkey, before, out, far_turned, *refs):
    results, (lcol, racc) = refs[:returns], refs[returns:]
    me = lax.axis_index("blk")
    out[...] = before[...]
    with_early(me, early, far, turned, lkey, lcol, racc, out)

    @pl.when(early[me, 1] > 0)
    def _():
        flush(racc, out, early[me, 0])

    @pl.when(meets[me, 0] > 0)
    def _():
        turn(far, far_turned)

    give(out, back, results)


def last_kernel(returns, early, meets, back, block, far, far_other, turned, far_turned, lkey, before, mine, *refs):
    results, (out, lcol, racc, other_turned, fkey) = refs[:returns], refs[returns:]
    rows = racc.shape[0]
    me = lax.axis_index("blk")
    out[...] = before[...]
    with_early(me, early, block, turned, lkey, lcol, racc, out)

    @pl.when(meets[me, 0] > 0)
    def _():
        fkey[...] = column_labels(far, rows)
        tile(block[:rows, :], far_turned, lcol, fkey, racc, out, meets[me, 2], False)

    @pl.when(meets[me, 1] > 0)
    def _():
        fkey[...] = column_labels(far_other, rows)
        turn(far_other, other_turned)
        tile(block[:rows, :], other_turned, lcol, fkey, racc, out, meets[me, 3], False)

    flush(racc, out, early[me, 0])
    mine[...] = out[me]
    give(out, back, results)


def run(stage, kernel, tables, operands, out_shape, scratch):
    vmem = pl.BlockSpec(memory_space=pltpu.VMEM)
    smem = pl.BlockSpec(memory_space=pltpu.SMEM)
    rows = out_shape[0].shape[-1]
    one = jax.ShapeDtypeStruct((1, rows), jnp.float32)
    returns = len(BACK[stage])
    tables = [jnp.asarray(t) for t in (*tables, np.array(BACK[stage] + ((0,) * N,), np.int32).T)]
    out_shape = out_shape + [one] * returns
    got = pl.pallas_call(
        functools.partial(kernel, returns),
        out_shape=out_shape,
        in_specs=[smem] * 3 + [vmem] * len(operands),
        out_specs=[vmem] * len(out_shape),
        scratch_shapes=scratch,
        compiler_params=pltpu.CompilerParams(vmem_limit_bytes=20 * 2 ** 20),
        cost_estimate=pl.CostEstimate(flops=COST[stage], bytes_accessed=0, transcendentals=0),
    )(*tables, *operands)
    return got[:len(got) - returns], got[len(got) - returns:]


def shards(embeddings, cluster_ids, valid):
    me = lax.axis_index("blk")
    move = functools.partial(lax.ppermute, axis_name="blk")
    mine, mine_x = pack(embeddings, cluster_ids, valid)
    near = move(mine, perm=ALONG)
    far = move(mine_x, perm=ACROSS)
    other = move(mine, perm=BUDDY)
    second = move(jnp.where((sum(p << d for d, p in enumerate(PASSES_ON)) >> me) & 1 > 0, near, other), perm=ALONG)
    near_other = move(near, perm=BUDDY)
    blocks = [mine, other, near, near_other]
    rows, depth = embeddings.shape
    maxima = jax.ShapeDtypeStruct((N, 1, rows), jnp.float32)
    one = jax.ShapeDtypeStruct((1, rows), jnp.float32)
    turned = jax.ShapeDtypeStruct((depth, rows), jnp.bfloat16)
    by_row = pltpu.VMEM((rows, 128), jnp.float32)
    use, pairs = first_schedule()
    (got, early, keys), back = run(
        0, functools.partial(first_kernel, pairs.shape[1] // FIELDS), (use, pairs), blocks,
        [maxima, jax.ShapeDtypeStruct((4, depth, rows), jnp.bfloat16), jax.ShapeDtypeStruct((4, 8, rows), jnp.float32)],
        [pltpu.VMEM((4, rows, depth), jnp.bfloat16), pltpu.VMEM((4, rows, 128), jnp.float32), by_row])
    far, got = lax.optimization_barrier((far, got))
    far_other = move(far, perm=[(d, t) for d, t in BUDDY if d // 2 in LATE])
    (got, far_turned), more = run(
        1, second_kernel, (late_schedule(1, 4)[0], late_schedule(2, 6)[1]), [far, early, keys, got],
        [maxima, turned], [by_row, by_row])
    second, got = lax.optimization_barrier((second, got))
    (result,), last = run(
        2, last_kernel, late_schedule(2, 6), [second, far, far_other, early, far_turned, keys, got],
        [one], [pltpu.VMEM(maxima.shape, jnp.float32), by_row, by_row,
                pltpu.VMEM(turned.shape, jnp.bfloat16), pltpu.VMEM((8, rows), jnp.float32)])
    for rows, row in zip([*back, *more, *last], sum(BACK, ())):
        result = jnp.maximum(result, move(rows, perm=full(row)))
    return result.reshape(-1)


def solution(mesh):
    return jax.shard_map(
        shards,
        mesh=mesh,
        in_specs=(P(("clus", "blk"), None), P(("clus", "blk")), P(("clus", "blk"))),
        out_specs=P(("clus", "blk")),
        check_vma=False,
    )
```

time: 178 us -> 63.7 us (0.36)
  waiting for transfers between devices: 111 us -> 24.6 us
  blocking collectives: 25.9 us -> 0 us
  matrix products: 21.9 us -> 0 us
  starting transfers between devices: 0.01 us -> 20.7 us
  Pallas kernels: 0 us -> 17.3 us
  between operations: 13.4 us -> 0.15 us
  other arithmetic: 5.62 us -> 0.75 us
    all_gather x1 -> x0, waiting for transfers between devices: 111 us -> none  [shards(): piece = lax.all_gather(unit, 'blk', axis=0, tiled=True)]
    all_gather x1 -> x0, blocking collectives: 25.9 us -> none  [shards(): all_labels = lax.all_gather(label, 'blk', axis=0, tiled=True)]
    ppermute x0 -> x11, waiting for transfers between devices: none -> 24.6 us  [the longest x1 12.5 us: shards(): near = move(mine, perm=ALONG)]
    dot_general x1 -> x0, matrix products: 21.9 us -> none  [masked_tile(): scores = jnp.dot(query, keys.T, preferred_element_type=jnp.float32)]
    ppermute x0 -> x11, starting transfers between devices: none -> 20.7 us  [the longest x5 9.66 us: shards(): result = jnp.maximum(result, move(rows, perm=full(row)))]
    pallas_call x0 -> x4, Pallas kernels: none -> 17.3 us  [the longest x3 14.5 us: run(): pl.pallas_call(functools.partial(kernel, returns), out_shape=out_shape, i...]
    convert_element_type x1 -> x0, other arithmetic: 2.66 us -> none  [normalize(): return (values * scale[:, None]).astype(jnp.bfloat16)]
  transfers between devices with their start and end apart: 1 -> 11, of which waited for: 1 -> 5; matrix products, arithmetic and copies ran while one was open for 0% -> 0% of each run, Pallas kernels for 0% -> 23%
where the time goes in v1:
time: 63.7 us; the launch traced here: 63.5 us
  waiting for transfers between devices  24.6 us (39%)
  starting transfers between devices  20.7 us (32%)
  Pallas kernels  17.3 us (27%)
  other arithmetic  0.75 us (1%)
    pallas_call x3, Pallas kernels, run(): pl.pallas_call(functools.partial(kernel, returns), out_shape=out_shape, i...  14.5 us
    ppermute x1, waiting for transfers between devices, shards(): near = move(mine, perm=ALONG)  12.5 us
    ppermute x5, starting transfers between devices, shards(): result = jnp.maximum(result, move(rows, perm=full(row)))  9.66 us
    ppermute x1, waiting for transfers between devices, shards(): far = move(mine_x, perm=ACROSS)  5.59 us
    ppermute x5, waiting for transfers between devices, shards(): result = jnp.maximum(result, move(rows, perm=full(row)))  3.92 us
    ppermute x1, starting transfers between devices, shards(): near_other = move(near, perm=BUDDY)  3.84 us
    ppermute x1, starting transfers between devices, shards(): near = move(mine, perm=ALONG)  3.64 us
    pallas_call x1, Pallas kernels, pack(): pl.pallas_call(pack_kernel, out_shape=[jax.ShapeDtypeStruct((rows + n * P...  2.77 us
  transfers between devices with their start and end apart: 11, of which 5 were waited for; matrix products, arithmetic and copies ran while one was open for 0% of the time, Pallas kernels for 23%

profile of v1, /device:TPU:1, one launch (start us, length us, event | category | flops | bytes accessed | tf_op | source)
XLA Modules:
  0.0 63.5 jit_solution(6867749943856016113)
XLA Ops:
  0.0 2.8 %shard_map.118 = (bf16[656,1024]{1,0:T(8,128)(2,1)}, bf16[672,1024]{1,0:T(8,128)(2,1)}) custom-call(s32[640]{0:T(1024)} %ids_in.1, s32[640]{0:T(1024)} %valid_in.1, bf16[640,1024]{1,0:T(8,128)(2,1)} %rows_in.1), custom_call_target="tpu_custom_call" | custom-call | flops 2621440 | bytes 2621440 | tf_op jit(solution)/shard_map/pallas_call | solution.py:186
  2.8 3.6 %collective-permute-start = (bf16[656,1024]{1,0:T(8,128)(2,1)}, bf16[656,1024]{1,0:T(8,128)(2,1)S(1)}, u32[]{:S(2)}, u32[]{:S(2)}) collective-permute-start(bf16[656,1024]{1,0:T(8,128)(2,1)} %get-tuple-element.22.refs_0_), channel_id=1, source_target_pairs={{0,2},{2,4},{4,6},{6,0},{8,10},{10,12},{12,14},{14,8},{1,7},{3,1},... | collective-permute-start | bytes 4030472 | tf_op jit(solution)/shard_map/ppermute | solution.py:390
  6.4 2.7 %collective-permute-start.3 = (bf16[672,1024]{1,0:T(8,128)(2,1)}, bf16[672,1024]{1,0:T(8,128)(2,1)}, u32[]{:S(2)}, u32[]{:S(2)}) collective-permute-start(bf16[672,1024]{1,0:T(8,128)(2,1)} %get-tuple-element.23), channel_id=1, source_target_pairs={{0,8},{1,9},{2,10},{3,11},{4,12},{5,13},{6,14},{7,15},{8,0},{9,1},... | collective-permute-start | bytes 4128776 | tf_op jit(solution)/shard_map/ppermute | solution.py:391
  9.2 12.5 %collective-permute-done.refs_2_ = bf16[656,1024]{1,0:T(8,128)(2,1)S(1)} collective-permute-done((bf16[656,1024]{1,0:T(8,128)(2,1)}, bf16[656,1024]{1,0:T(8,128)(2,1)S(1)}, u32[]{:S(2)}, u32[]{:S(2)}) %collective-permute-start) | collective-permute-done | bytes 1343520 | tf_op jit(solution)/shard_map/ppermute | solution.py:390
  21.6 3.8 %collective-permute-start.4 = (bf16[656,1024]{1,0:T(8,128)(2,1)S(1)}, bf16[656,1024]{1,0:T(8,128)(2,1)}, u32[]{:S(2)}, u32[]{:S(2)}) collective-permute-start(bf16[656,1024]{1,0:T(8,128)(2,1)S(1)} %collective-permute-done.refs_2_), channel_id=1, source_target_pairs={{0,1},{1,0},{2,3},{3,2},{4,5},{5,4},{6,7},{7,6},{8,9},{9,8},{10,11... | collective-permute-start | bytes 4030472 | tf_op jit(solution)/shard_map/ppermute | solution.py:394
  25.5 0.1 broadcast_select_fusion
  25.6 0.1 collective-permute-start.2
  25.7 2.6 %collective-permute-done.4.refs_3_ = bf16[656,1024]{1,0:T(8,128)(2,1)} collective-permute-done((bf16[656,1024]{1,0:T(8,128)(2,1)S(1)}, bf16[656,1024]{1,0:T(8,128)(2,1)}, u32[]{:S(2)}, u32[]{:S(2)}) %collective-permute-start.4) | collective-permute-done | bytes 1343520 | tf_op jit(solution)/shard_map/ppermute | solution.py:394
  28.3 0.0 copy-start.3
  28.3 0.0 copy-start.6
  28.4 0.0 copy-start.7
  28.4 5.5 %shard_map.119 = (f32[16,1,640]{2,1,0:T(1,128)S(1)}, bf16[4,1024,640]{2,1,0:T(8,128)(2,1)S(1)}, f32[4,8,640]{2,1,0:T(8,128)S(1)}) custom-call(s32[16,4]{1,0:T(8,128)S(1)} %copy-done.1, s32[16,15]{1,0:T(8,128)S(1)} %copy-done.2, s32[16,1]{1,0:T(8,128)S(1)} %call_exported.0.back, bf16[656,1024]{1,0:T(8,128)(2,1)S(1)} %copy-done, ...), custom_call_target="tpu_custom_call" | custom-call | tf_op jit(solution)/shard_map/pallas_call | solution.py:374
  33.9 5.6 %collective-permute-done.3.far = bf16[672,1024]{1,0:T(8,128)(2,1)} collective-permute-done((bf16[672,1024]{1,0:T(8,128)(2,1)}, bf16[672,1024]{1,0:T(8,128)(2,1)}, u32[]{:S(2)}, u32[]{:S(2)}) %collective-permute-start.3) | collective-permute-done | bytes 1376288 | tf_op jit(solution)/shard_map/ppermute | solution.py:391
  39.5 0.7 %collective-permute-start.5 = (bf16[672,1024]{1,0:T(8,128)(2,1)}, bf16[672,1024]{1,0:T(8,128)(2,1)S(1)}, u32[]{:S(2)}, u32[]{:S(2)}) collective-permute-start(bf16[672,1024]{1,0:T(8,128)(2,1)} %collective-permute-done.3.far), channel_id=1, source_target_pairs={{12,13},{13,12},{14,15},{15,14},{28,29},{29,28},{30,31},{31,30},{4... | collective-permute-start | bytes 4128776 | tf_op jit(solution)/shard_map/ppermute | solution.py:407
  40.3 4.7 %shard_map.120 = (f32[16,1,640]{2,1,0:T(1,128)S(1)}, bf16[1024,640]{1,0:T(8,128)(2,1)S(1)}, f32[1,640]{1,0:T(1,128)S(1)}, f32[1,640]{1,0:T(1,128)S(1)}) custom-call(s32[16,14]{1,0:T(8,128)S(1)} %copy-done.6, s32[16,4]{1,0:T(8,128)S(1)} %copy-done.3, s32[16,3]{1,0:T(8,128)S(1)} %copy-done.7, bf16[672,1024]{1,0:T(8,128)(2,1)} %collective-permute-done.3.far, ...), custom_call_target="tpu_custom_call" | custom-call | flops 20000000000 | tf_op jit(solution)/shard_map/pallas_call | solution.py:374
  45.0 6.0 %collective-permute-start.6 = (f32[1,640]{1,0:T(1,128)S(1)}, f32[1,640]{1,0:T(1,128)S(1)}, u32[]{:S(2)}, u32[]{:S(2)}) collective-permute-start(f32[1,640]{1,0:T(1,128)S(1)} %get-tuple-element.34), channel_id=1, source_target_pairs={{0,1},{1,15},{2,0},{3,14},{4,5},{5,2},{6,7},{7,4},{8,12},{9,11},{1... | collective-permute-start | bytes 7688 | tf_op jit(solution)/shard_map/ppermute | solution.py:417
  51.0 0.3 collective-permute-start.7
  51.3 4.3 %shard_map.121 = (f32[1,640]{1,0:T(1,128)S(1)}, f32[1,640]{1,0:T(1,128)S(1)}, f32[1,640]{1,0:T(1,128)S(1)}, f32[1,640]{1,0:T(1,128)S(1)}) custom-call(s32[16,14]{1,0:T(8,128)S(1)} %copy-done.4, s32[16,4]{1,0:T(8,128)S(1)} %copy-done.3, s32[16,4]{1,0:T(8,128)S(1)} %copy-done.5, bf16[656,1024]{1,0:T(8,128)(2,1)S(1)} %collective-permute-done.2.block, ...), custom_call_target="tpu_custom_call" | custom-call | tf_op jit(solution)/shard_map/pallas_call | solution.py:374
  55.6 0.1 collective-permute-start.10
  55.7 3.0 %collective-permute-start.8 = (f32[1,640]{1,0:T(1,128)S(1)}, f32[1,640]{1,0:T(1,128)S(1)}, u32[]{:S(2)}, u32[]{:S(2)}) collective-permute-start(f32[1,640]{1,0:T(1,128)S(1)} %get-tuple-element.36), channel_id=1, source_target_pairs={{0,3},{1,9},{2,10},{3,0},{4,12},{5,15},{6,14},{7,1},{8,11},{9,13},... | collective-permute-start | bytes 7688 | tf_op jit(solution)/shard_map/ppermute | solution.py:417
  58.7 0.3 collective-permute-start.9
  59.0 0.9 %collective-permute-done.10 = f32[1,640]{1,0:T(1,128)S(1)} collective-permute-done((f32[1,640]{1,0:T(1,128)S(1)}, f32[1,640]{1,0:T(1,128)S(1)}, u32[]{:S(2)}, u32[]{:S(2)}) %collective-permute-start.10) | collective-permute-done | bytes 2592 | tf_op jit(solution)/shard_map/ppermute | solution.py:417
  59.9 3.0 %collective-permute-done.9 = f32[1,640]{1,0:T(1,128)S(1)} collective-permute-done((f32[1,640]{1,0:T(1,128)S(1)}, f32[1,640]{1,0:T(1,128)S(1)}, u32[]{:S(2)}, u32[]{:S(2)}) %collective-permute-start.9) | collective-permute-done | bytes 2592 | tf_op jit(solution)/shard_map/ppermute | solution.py:417
  62.9 0.6 maximum_reduce_fusion
  (21 shorter events, 0.1 us)
Async XLA Ops:
  2.8 18.9 %collective-permute-start = (bf16[656,1024]{1,0:T(8,128)(2,1)}, bf16[656,1024]{1,0:T(8,128)(2,1)S(1)}, u32[]{:S(2)}, u32[]{:S(2)}) collective-permute-start(bf16[656,1024]{1,0:T(8,128)(2,1)} %get-tuple-element.22.refs_0_), channel_id=1, source_target_pairs={{0,2},{2,4},{4,6},{6,0},{8,10},{10,12},{12,14},{14,8},{1,7},{3,1},... | collective-permute-start | bytes 4030472 | tf_op jit(solution)/shard_map/ppermute | solution.py:390
  6.4 19.1 %collective-permute-start.1 = (bf16[656,1024]{1,0:T(8,128)(2,1)}, bf16[656,1024]{1,0:T(8,128)(2,1)S(1)}, u32[]{:S(2)}, u32[]{:S(2)}) collective-permute-start(bf16[656,1024]{1,0:T(8,128)(2,1)} %get-tuple-element.22.refs_0_), channel_id=1, source_target_pairs={{0,1},{1,0},{2,3},{3,2},{4,5},{5,4},{6,7},{7,6},{8,9},{9,8},{10,11... | collective-permute-start | bytes 4030472 | tf_op jit(solution)/shard_map/ppermute | solution.py:392
  6.4 33.1 %collective-permute-start.3 = (bf16[672,1024]{1,0:T(8,128)(2,1)}, bf16[672,1024]{1,0:T(8,128)(2,1)}, u32[]{:S(2)}, u32[]{:S(2)}) collective-permute-start(bf16[672,1024]{1,0:T(8,128)(2,1)} %get-tuple-element.23), channel_id=1, source_target_pairs={{0,8},{1,9},{2,10},{3,11},{4,12},{5,13},{6,14},{7,15},{8,0},{9,1},... | collective-permute-start | bytes 4128776 | tf_op jit(solution)/shard_map/ppermute | solution.py:391
  21.6 6.7 %collective-permute-start.4 = (bf16[656,1024]{1,0:T(8,128)(2,1)S(1)}, bf16[656,1024]{1,0:T(8,128)(2,1)}, u32[]{:S(2)}, u32[]{:S(2)}) collective-permute-start(bf16[656,1024]{1,0:T(8,128)(2,1)S(1)} %collective-permute-done.refs_2_), channel_id=1, source_target_pairs={{0,1},{1,0},{2,3},{3,2},{4,5},{5,4},{6,7},{7,6},{8,9},{9,8},{10,11... | collective-permute-start | bytes 4030472 | tf_op jit(solution)/shard_map/ppermute | solution.py:394
  25.5 2.8 %copy-start = (bf16[656,1024]{1,0:T(8,128)(2,1)S(1)}, bf16[656,1024]{1,0:T(8,128)(2,1)}, u32[]{:S(2)}) copy-start(bf16[656,1024]{1,0:T(8,128)(2,1)} %get-tuple-element.22.refs_0_) | copy-start | bytes 4030468
  25.5 2.8 %copy-start.1 = (s32[16,4]{1,0:T(8,128)S(1)}, s32[16,4]{1,0:T(8,128)}, u32[]{:S(2)}) copy-start(s32[16,4]{1,0:T(8,128)} %constant.26.clone.use) | copy-start | bytes 772
  25.5 2.8 %copy-start.2 = (s32[16,15]{1,0:T(8,128)S(1)}, s32[16,15]{1,0:T(8,128)}, u32[]{:S(2)}) copy-start(s32[16,15]{1,0:T(8,128)} %constant.27.clone.pairs) | copy-start | bytes 2884
  25.6 19.4 %collective-permute-start.2 = (bf16[656,1024]{1,0:T(8,128)(2,1)S(1)}, bf16[656,1024]{1,0:T(8,128)(2,1)S(1)}, u32[]{:S(2)}, u32[]{:S(2)}) collective-permute-start(bf16[656,1024]{1,0:T(8,128)(2,1)S(1)} %broadcast_select_fusion), channel_id=1, source_target_pairs={{0,2},{2,4},{4,6},{6,0},{8,10},{10,12},{12,14},{14,8},{1,7},{3,1},... | collective-permute-start | bytes 4030472 | tf_op jit(solution)/shard_map/ppermute | solution.py:393
  28.3 11.9 %copy-start.3 = (s32[16,4]{1,0:T(8,128)S(1)}, s32[16,4]{1,0:T(8,128)}, u32[]{:S(2)}) copy-start(s32[16,4]{1,0:T(8,128)} %constant.30.clone.meets) | copy-start | bytes 772
  28.3 11.9 %copy-start.6 = (s32[16,14]{1,0:T(8,128)S(1)}, s32[16,14]{1,0:T(8,128)}, u32[]{:S(2)}) copy-start(s32[16,14]{1,0:T(8,128)} %constant.29.clone.early) | copy-start | bytes 2692
  28.4 11.9 %copy-start.7 = (s32[16,3]{1,0:T(8,128)S(1)}, s32[16,3]{1,0:T(8,128)}, u32[]{:S(2)}) copy-start(s32[16,3]{1,0:T(8,128)} %constant.31.clone.back) | copy-start | bytes 580
  39.5 11.9 %collective-permute-start.5 = (bf16[672,1024]{1,0:T(8,128)(2,1)}, bf16[672,1024]{1,0:T(8,128)(2,1)S(1)}, u32[]{:S(2)}, u32[]{:S(2)}) collective-permute-start(bf16[672,1024]{1,0:T(8,128)(2,1)} %collective-permute-done.3.far), channel_id=1, source_target_pairs={{12,13},{13,12},{14,15},{15,14},{28,29},{29,28},{30,31},{31,30},{4... | collective-permute-start | bytes 4128776 | tf_op jit(solution)/shard_map/ppermute | solution.py:407
  40.3 11.1 %copy-start.4 = (s32[16,14]{1,0:T(8,128)S(1)}, s32[16,14]{1,0:T(8,128)}, u32[]{:S(2)}) copy-start(s32[16,14]{1,0:T(8,128)} %constant.32.clone.early) | copy-start | bytes 2692
  40.3 11.1 %copy-start.5 = (s32[16,4]{1,0:T(8,128)S(1)}, s32[16,4]{1,0:T(8,128)}, u32[]{:S(2)}) copy-start(s32[16,4]{1,0:T(8,128)} %constant.33.clone.back) | copy-start | bytes 772
  45.0 14.0 %collective-permute-start.6 = (f32[1,640]{1,0:T(1,128)S(1)}, f32[1,640]{1,0:T(1,128)S(1)}, u32[]{:S(2)}, u32[]{:S(2)}) collective-permute-start(f32[1,640]{1,0:T(1,128)S(1)} %get-tuple-element.34), channel_id=1, source_target_pairs={{0,1},{1,15},{2,0},{3,14},{4,5},{5,2},{6,7},{7,4},{8,12},{9,11},{1... | collective-permute-start | bytes 7688 | tf_op jit(solution)/shard_map/ppermute | solution.py:417
  51.0 8.0 %collective-permute-start.7 = (f32[1,640]{1,0:T(1,128)S(1)}, f32[1,640]{1,0:T(1,128)S(1)}, u32[]{:S(2)}, u32[]{:S(2)}) collective-permute-start(f32[1,640]{1,0:T(1,128)S(1)} %get-tuple-element.35), channel_id=1, source_target_pairs={{0,6},{1,14},{2,3},{3,5},{4,11},{5,7},{6,4},{7,2},{8,0},{9,8},{10,... | collective-permute-start | bytes 7688 | tf_op jit(solution)/shard_map/ppermute | solution.py:417
  55.6 4.3 %collective-permute-start.10 = (f32[1,640]{1,0:T(1,128)S(1)}, f32[1,640]{1,0:T(1,128)S(1)}, u32[]{:S(2)}, u32[]{:S(2)}) collective-permute-start(f32[1,640]{1,0:T(1,128)S(1)} %get-tuple-element.38), channel_id=1, source_target_pairs={{0,7},{1,3},{2,13},{3,4},{4,2},{5,6},{6,5},{7,15},{8,14},{9,1},{10... | collective-permute-start | bytes 7688 | tf_op jit(solution)/shard_map/ppermute | solution.py:417
  55.7 4.2 %collective-permute-start.8 = (f32[1,640]{1,0:T(1,128)S(1)}, f32[1,640]{1,0:T(1,128)S(1)}, u32[]{:S(2)}, u32[]{:S(2)}) collective-permute-start(f32[1,640]{1,0:T(1,128)S(1)} %get-tuple-element.36), channel_id=1, source_target_pairs={{0,3},{1,9},{2,10},{3,0},{4,12},{5,15},{6,14},{7,1},{8,11},{9,13},... | collective-permute-start | bytes 7688 | tf_op jit(solution)/shard_map/ppermute | solution.py:417
  58.7 4.2 %collective-permute-start.9 = (f32[1,640]{1,0:T(1,128)S(1)}, f32[1,640]{1,0:T(1,128)S(1)}, u32[]{:S(2)}, u32[]{:S(2)}) collective-permute-start(f32[1,640]{1,0:T(1,128)S(1)} %get-tuple-element.37), channel_id=1, source_target_pairs={{0,8},{1,2},{2,6},{3,11},{4,3},{5,13},{6,1},{7,0},{8,15},{9,14},{1... | collective-permute-start | bytes 7688 | tf_op jit(solution)/shard_map/ppermute | solution.py:417

commit v2 on v1

--- a/solution.py
+++ b/solution.py
@@ -11,7 +11,7 @@
 N = 16
 PAD = 16
 
-MODE = (1, 0, 0, 0, 2, 3, 1, 2)
+MODE = (3, 0, 0, 0, 3, 3, 1, 2)
 
 
 def up(chip):
@@ -45,54 +45,50 @@
 LATE = (6, 7)
 
 WORK = (
-    [[[(0, 1), (0, 6), (3, 6)], [(1, 8), (6, 8)], [(3, 7), (7, 8)]],
-     [[(1, 3)], [(1, 9), (3, 9)], [(1, 2), (2, 9)]],
-     [[(0, 2), (2, 3)], [], [(2, 6), (6, 10)]],
-     [[(0, 3), (0, 5), (3, 5)], [(3, 11), (5, 11)], [(0, 4), (4, 11)]],
-     [[(2, 4), (2, 5), (4, 5)], [(5, 12)], [(3, 4)]],
-     [[(2, 7), (5, 7)], [(5, 13), (7, 13)], [(6, 13)]],
-     [[(1, 6), (4, 6), (6, 7)], [(6, 14), (7, 14)], [(1, 5), (5, 6)]],
-     [[(1, 4), (1, 7), (4, 7)], [(7, 15)], [(0, 7)]],
+    [[[(1, 3)], [(1, 8), (6, 8)], [(0, 7), (7, 8)]],
+     [[(0, 1), (0, 6), (3, 6)], [(3, 9), (6, 9)], [(1, 2), (2, 9)]],
+     [[(0, 2), (2, 5), (3, 5)], [], [(6, 10)]],
+     [[(0, 3), (0, 5), (2, 3)], [(3, 11), (5, 11)], [(0, 4), (4, 11)]],
+     [[(2, 4), (2, 7), (5, 7)], [(7, 12)], [(3, 4), (3, 7)]],
+     [[(4, 5), (4, 7)], [(5, 13), (7, 13)], [(2, 6), (6, 13)]],
+     [[(1, 4), (4, 6), (6, 7)], [], [(1, 5), (5, 6)]],
+     [[(1, 6), (1, 7)], [(7, 15)], []],
      [[(8, 11), (8, 14), (11, 14)], [(0, 8)], [(8, 15), (11, 15)]],
-     [[(8, 9), (9, 11), (9, 14)], [], [(9, 13), (13, 14)]],
-     [[(8, 10)], [(2, 8), (2, 10)], [(9, 10)]],
-     [[(8, 13), (10, 11), (11, 13)], [(3, 8), (3, 10)], [(8, 12), (11, 12)]],
-     [[(10, 12), (12, 13)], [(4, 10), (4, 12)], [(4, 8), (5, 8)]],
-     [[(10, 13), (10, 15), (13, 15)], [(5, 10)], [(4, 9), (5, 9)]],
-     [[(9, 12), (12, 14), (14, 15)], [(6, 9), (6, 12)], [(7, 10), (10, 14)]],
-     [[(9, 15), (12, 15), (14, 15)], [(7, 9), (7, 12)], [(6, 11), (7, 11)]]])
+     [[(8, 9), (9, 11), (9, 14)], [(1, 9)], [(9, 13), (13, 14)]],
+     [[(8, 13), (11, 13)], [(2, 8), (2, 10)], [(10, 14)]],
+     [[(8, 10), (10, 11), (10, 13)], [(3, 8), (3, 10)], [(8, 12), (11, 12)]],
+     [[(12, 13), (12, 15), (13, 15)], [(4, 10), (4, 12)], [(4, 8), (5, 8)]],
+     [[(10, 12), (10, 15)], [(5, 10), (5, 12)], [(4, 9), (5, 9)]],
+     [[(9, 12)], [(6, 12), (6, 14)], [(7, 10), (9, 10)]],
+     [[(9, 15), (12, 14), (14, 15)], [(7, 9), (7, 14)], [(6, 11), (7, 11)]]])
 
 BACK = (
-    (),
-    (
-        (1, -1, 0, -1, 5, 2, 7, 4, -1, 11, 8, 3, 13, 10, 6, 9),
-        (6, -1, 3, 5, -1, 7, 4, -1, 0, 8, -1, 13, 10, 15, 9, 12),
-    ),
-    (
-        (3, 9, 10, 0, 12, -1, 14, 1, 11, 13, 2, 8, 5, 4, 7, 6),
-        (8, 2, 6, 11, 3, 13, 1, 0, 15, 14, 9, 10, 4, 5, 12, 7),
-        (7, 3, -1, 4, 2, 6, 5, 15, 14, -1, -1, 12, 8, 9, 10, 11),
-    ),
+    (4, 5, -1, 0, 6, 7, 2, 3),
+    (1, 0, 3, 2, 5, 6, 7, 4),
+    (3, 2, 6, 7, 0, 1, 4, 5),
+    (-1, 3, 1, -1, 7, 4, 5, 6),
 )
 
 
 def check():
     served = set()
     for d in range(N):
-        for stage, pairs in enumerate(WORK[d]):
-            for a, b in pairs:
-                for owner, partner in ((a, b), (b, a)):
-                    if owner == d or any(row[d] == owner for later in BACK[stage:] for row in later):
-                        served.add((owner, partner))
+        for a, b in sum(WORK[d], []):
+            for owner, partner in ((a, b), (b, a)):
+                if owner // 2 == d // 2 or any(row[d // 2] == owner // 2 for row in BACK):
+                    served.add((owner, partner))
     assert all((a, b) in served for a in range(N) for b in range(N) if 0 < abs(a - b) <= 8)
 
 
 check()
 
 
-def full(row):
-    free = [t for t in range(N) if t not in row]
-    return [(d, t if t >= 0 else free.pop()) for d, t in enumerate(row)]
+def sends(pair):
+    moves = []
+    for core, row in enumerate(pair):
+        free = [t for t in range(N // 2) if t not in row]
+        moves += [(2 * c + core, 2 * (t if t >= 0 else free.pop()) + core) for c, t in enumerate(row)]
+    return moves
 
 
 def grouped(pairs, lead):
@@ -108,7 +104,6 @@
 
 FIELDS = 5
 LATER = 6
-COST = (0, 2 * 10 ** 10, 0)
 
 
 def first_schedule():
@@ -256,16 +251,26 @@
     racc[...] = jnp.full_like(racc, -1.0)
 
 
-def give(out, back, results):
+def merge_kernel(targets, out, other, mine, *sent):
     me = lax.axis_index("blk")
-    for k, result in enumerate(results):
-        to = back[me, k]
-        result[...] = jnp.where(to >= 0, out[jnp.maximum(to, 0)], -1.0)
-
-
-def first_kernel(count, returns, use, pairs, back, *refs):
-    blocks, (out, turned, lkey), results = refs[:4], refs[4:7], refs[7:7 + returns]
-    unit, lcol, racc = refs[7 + returns:]
+    for n in (0, 1):
+        at = me // 2 * 2 + n
+        mine[n] = jnp.maximum(out[at], other[at])
+        for k, ref in enumerate(sent):
+            to = targets[me, k]
+            at = jnp.maximum(to, 0) * 2 + n
+            ref[n] = jnp.where(to >= 0, jnp.maximum(out[at], other[at]), -1.0)
+
+
+def split_kernel(*refs):
+    *found, keep, pass_on = refs
+    core = lax.axis_index("blk") % 2
+    for ref, at in ((keep, core), (pass_on, 1 - core)):
+        ref[...] = functools.reduce(jnp.maximum, [f[at] for f in found])
+
+
+def first_kernel(count, use, pairs, *refs):
+    blocks, (out, turned, lkey), (unit, lcol, racc) = refs[:4], refs[4:7], refs[7:]
     rows = racc.shape[0]
     me = lax.axis_index("blk")
     out[...] = jnp.full_like(out, -1.0)
@@ -307,7 +312,6 @@
         return 0
 
     lax.fori_loop(0, count, each, 0)
-    give(out, back, results)
 
 
 def with_early(me, early, block, turned, lkey, lcol, racc, out):
@@ -323,8 +327,7 @@
     lax.fori_loop(0, early[me, 1], each, 0)
 
 
-def second_kernel(returns, early, meets, back, far, turned, lkey, before, out, far_turned, *refs):
-    results, (lcol, racc) = refs[:returns], refs[returns:]
+def second_kernel(early, meets, far, turned, lkey, before, out, far_turned, fkey, lcol, racc):
     me = lax.axis_index("blk")
     out[...] = before[...]
     with_early(me, early, far, turned, lkey, lcol, racc, out)
@@ -335,13 +338,11 @@
 
     @pl.when(meets[me, 0] > 0)
     def _():
+        fkey[...] = column_labels(far, racc.shape[0])
         turn(far, far_turned)
 
-    give(out, back, results)
-
-
-def last_kernel(returns, early, meets, back, block, far, far_other, turned, far_turned, lkey, before, mine, *refs):
-    results, (out, lcol, racc, other_turned, fkey) = refs[:returns], refs[returns:]
+
+def last_kernel(early, meets, block, far_other, turned, far_turned, fkey, lkey, before, out, lcol, racc, other_turned, okey):
     rows = racc.shape[0]
     me = lax.axis_index("blk")
     out[...] = before[...]
@@ -349,38 +350,29 @@
 
     @pl.when(meets[me, 0] > 0)
     def _():
-        fkey[...] = column_labels(far, rows)
         tile(block[:rows, :], far_turned, lcol, fkey, racc, out, meets[me, 2], False)
 
     @pl.when(meets[me, 1] > 0)
     def _():
-        fkey[...] = column_labels(far_other, rows)
+        okey[...] = column_labels(far_other, rows)
         turn(far_other, other_turned)
-        tile(block[:rows, :], other_turned, lcol, fkey, racc, out, meets[me, 3], False)
+        tile(block[:rows, :], other_turned, lcol, okey, racc, out, meets[me, 3], False)
 
     flush(racc, out, early[me, 0])
-    mine[...] = out[me]
-    give(out, back, results)
-
-
-def run(stage, kernel, tables, operands, out_shape, scratch):
+
+
+def run(kernel, tables, operands, out_shape, scratch=(), flops=0):
     vmem = pl.BlockSpec(memory_space=pltpu.VMEM)
     smem = pl.BlockSpec(memory_space=pltpu.SMEM)
-    rows = out_shape[0].shape[-1]
-    one = jax.ShapeDtypeStruct((1, rows), jnp.float32)
-    returns = len(BACK[stage])
-    tables = [jnp.asarray(t) for t in (*tables, np.array(BACK[stage] + ((0,) * N,), np.int32).T)]
-    out_shape = out_shape + [one] * returns
-    got = pl.pallas_call(
-        functools.partial(kernel, returns),
+    return pl.pallas_call(
+        kernel,
         out_shape=out_shape,
-        in_specs=[smem] * 3 + [vmem] * len(operands),
+        in_specs=[smem] * len(tables) + [vmem] * len(operands),
         out_specs=[vmem] * len(out_shape),
-        scratch_shapes=scratch,
-        compiler_params=pltpu.CompilerParams(vmem_limit_bytes=20 * 2 ** 20),
-        cost_estimate=pl.CostEstimate(flops=COST[stage], bytes_accessed=0, transcendentals=0),
-    )(*tables, *operands)
-    return got[:len(got) - returns], got[len(got) - returns:]
+        scratch_shapes=list(scratch),
+        compiler_params=pltpu.CompilerParams(vmem_limit_bytes=12 * 2 ** 20),
+        cost_estimate=pl.CostEstimate(flops=flops, bytes_accessed=0, transcendentals=0),
+    )(*[jnp.asarray(t) for t in tables], *operands)
 
 
 def shards(embeddings, cluster_ids, valid):
@@ -399,23 +391,25 @@
     turned = jax.ShapeDtypeStruct((depth, rows), jnp.bfloat16)
     by_row = pltpu.VMEM((rows, 128), jnp.float32)
     use, pairs = first_schedule()
-    (got, early, keys), back = run(
-        0, functools.partial(first_kernel, pairs.shape[1] // FIELDS), (use, pairs), blocks,
+    got, early, keys = run(
+        functools.partial(first_kernel, pairs.shape[1] // FIELDS), (use, pairs), blocks,
         [maxima, jax.ShapeDtypeStruct((4, depth, rows), jnp.bfloat16), jax.ShapeDtypeStruct((4, 8, rows), jnp.float32)],
         [pltpu.VMEM((4, rows, depth), jnp.bfloat16), pltpu.VMEM((4, rows, 128), jnp.float32), by_row])
     far, got = lax.optimization_barrier((far, got))
     far_other = move(far, perm=[(d, t) for d, t in BUDDY if d // 2 in LATE])
-    (got, far_turned), more = run(
-        1, second_kernel, (late_schedule(1, 4)[0], late_schedule(2, 6)[1]), [far, early, keys, got],
-        [maxima, turned], [by_row, by_row])
+    got, far_turned, far_keys = run(
+        second_kernel, (late_schedule(1, 4)[0], late_schedule(2, 6)[1]), [far, early, keys, got],
+        [maxima, turned, jax.ShapeDtypeStruct((8, rows), jnp.float32)], [by_row, by_row], flops=2 * 10 ** 10)
     second, got = lax.optimization_barrier((second, got))
-    (result,), last = run(
-        2, last_kernel, late_schedule(2, 6), [second, far, far_other, early, far_turned, keys, got],
-        [one], [pltpu.VMEM(maxima.shape, jnp.float32), by_row, by_row,
-                pltpu.VMEM(turned.shape, jnp.bfloat16), pltpu.VMEM((8, rows), jnp.float32)])
-    for rows, row in zip([*back, *more, *last], sum(BACK, ())):
-        result = jnp.maximum(result, move(rows, perm=full(row)))
-    return result.reshape(-1)
+    got, = run(
+        last_kernel, late_schedule(2, 6), [second, far_other, early, far_turned, far_keys, keys, got],
+        [maxima], [by_row, by_row, pltpu.VMEM(turned.shape, jnp.bfloat16), pltpu.VMEM((8, rows), jnp.float32)])
+    targets = np.array([[row[d // 2] for row in BACK[d % 2::2]] for d in range(N)], np.int32)
+    two = jax.ShapeDtypeStruct((2, 1, rows), jnp.float32)
+    mine, *sent = run(merge_kernel, (targets,), [got, move(got, perm=BUDDY)], [two] * (1 + len(BACK) // 2))
+    found = [mine] + [move(s, perm=sends(BACK[2 * k:2 * k + 2])) for k, s in enumerate(sent)]
+    keep, pass_on = run(split_kernel, (), found, [one] * 2)
+    return jnp.maximum(keep, move(pass_on, perm=BUDDY)).reshape(-1)
 
 
 def solution(mesh):

time: 63.7 us -> 62.6 us (0.983)
  Pallas kernels: 17.3 us -> 21.3 us
  waiting for transfers between devices: 24.6 us -> 20.6 us
  starting transfers between devices: 20.7 us -> 19.6 us
    pallas_call x3 -> x5, Pallas kernels: 14.5 us -> 18.5 us  [run(): pl.pallas_call(kernel, out_shape=out_shape, in_specs=[smem] * len(tables)...]
    ppermute x1, waiting for transfers between devices: 5.59 us -> 1.6 us  [shards(): far = move(mine_x, perm=ACROSS)]
    ppermute x5 -> x4, starting transfers between devices: 9.66 us -> 8.58 us  [the longest x1 5.26 us: shards(): return jnp.maximum(keep, move(pass_on, perm=BUDDY)).reshape(-1)]
    ppermute x5 -> x4, waiting for transfers between devices: 3.92 us -> 3.96 us  [the longest x2 2.26 us: shards(): move(s, perm=sends(BACK[2 * k:2 * k + 2]))]
  transfers between devices with their start and end apart: 11 -> 10, of which waited for: 5 -> 7; matrix products, arithmetic and copies ran while one was open for 0% -> 0% of each run, Pallas kernels for 23% -> 23%
where the time goes in v2:
time: 62.6 us; the launch traced here: 62.4 us
  Pallas kernels  21.3 us (34%)
  waiting for transfers between devices  20.6 us (33%)
  starting transfers between devices  19.6 us (31%)
  other arithmetic  0.75 us (1%)
    pallas_call x5, Pallas kernels, run(): pl.pallas_call(kernel, out_shape=out_shape, in_specs=[smem] * len(tables)...  18.5 us
    ppermute x1, waiting for transfers between devices, shards(): near = move(mine, perm=ALONG)  12.5 us
    ppermute x1, starting transfers between devices, shards(): return jnp.maximum(keep, move(pass_on, perm=BUDDY)).reshape(-1)  5.26 us
    ppermute x1, starting transfers between devices, shards(): near_other = move(near, perm=BUDDY)  3.84 us
    ppermute x1, starting transfers between devices, shards(): near = move(mine, perm=ALONG)  3.64 us
    pallas_call x1, Pallas kernels, pack(): pl.pallas_call(pack_kernel, out_shape=[jax.ShapeDtypeStruct((rows + n * P...  2.79 us
    ppermute x1, starting transfers between devices, shards(): far = move(mine_x, perm=ACROSS)  2.74 us
    ppermute x1, waiting for transfers between devices, shards(): near_other = move(near, perm=BUDDY)  2.56 us
  transfers between devices with their start and end apart: 10, of which 7 were waited for; matrix products, arithmetic and copies ran while one was open for 0% of the time, Pallas kernels for 23%

profile of v2, /device:TPU:1, one launch (start us, length us, event | category | flops | bytes accessed | tf_op | source)
XLA Modules:
  0.0 62.4 jit_solution(3068849355807176006)
XLA Ops:
  0.0 2.8 %shard_map.100 = (bf16[656,1024]{1,0:T(8,128)(2,1)}, bf16[672,1024]{1,0:T(8,128)(2,1)}) custom-call(s32[640]{0:T(1024)} %ids_in.1, s32[640]{0:T(1024)} %valid_in.1, bf16[640,1024]{1,0:T(8,128)(2,1)} %rows_in.1), custom_call_target="tpu_custom_call" | custom-call | flops 2621440 | bytes 2621440 | tf_op jit(solution)/shard_map/pallas_call | solution.py:181
  2.8 3.6 %collective-permute-start = (bf16[656,1024]{1,0:T(8,128)(2,1)}, bf16[656,1024]{1,0:T(8,128)(2,1)S(1)}, u32[]{:S(2)}, u32[]{:S(2)}) collective-permute-start(bf16[656,1024]{1,0:T(8,128)(2,1)} %get-tuple-element.22.refs_0_), channel_id=1, source_target_pairs={{0,2},{2,4},{4,6},{6,0},{8,10},{10,12},{12,14},{14,8},{1,7},{3,1},... | collective-permute-start | bytes 4030472 | tf_op jit(solution)/shard_map/ppermute | solution.py:382
  6.4 2.7 %collective-permute-start.3 = (bf16[672,1024]{1,0:T(8,128)(2,1)}, bf16[672,1024]{1,0:T(8,128)(2,1)}, u32[]{:S(2)}, u32[]{:S(2)}) collective-permute-start(bf16[672,1024]{1,0:T(8,128)(2,1)} %get-tuple-element.23), channel_id=1, source_target_pairs={{0,8},{1,9},{2,10},{3,11},{4,12},{5,13},{6,14},{7,15},{8,0},{9,1},... | collective-permute-start | bytes 4128776 | tf_op jit(solution)/shard_map/ppermute | solution.py:383
  9.2 12.5 %collective-permute-done.refs_2_ = bf16[656,1024]{1,0:T(8,128)(2,1)S(1)} collective-permute-done((bf16[656,1024]{1,0:T(8,128)(2,1)}, bf16[656,1024]{1,0:T(8,128)(2,1)S(1)}, u32[]{:S(2)}, u32[]{:S(2)}) %collective-permute-start) | collective-permute-done | bytes 1343520 | tf_op jit(solution)/shard_map/ppermute | solution.py:382
  21.7 3.8 %collective-permute-start.4 = (bf16[656,1024]{1,0:T(8,128)(2,1)S(1)}, bf16[656,1024]{1,0:T(8,128)(2,1)}, u32[]{:S(2)}, u32[]{:S(2)}) collective-permute-start(bf16[656,1024]{1,0:T(8,128)(2,1)S(1)} %collective-permute-done.refs_2_), channel_id=1, source_target_pairs={{0,1},{1,0},{2,3},{3,2},{4,5},{5,4},{6,7},{7,6},{8,9},{9,8},{10,11... | collective-permute-start | bytes 4030472 | tf_op jit(solution)/shard_map/ppermute | solution.py:386
  25.5 0.1 broadcast_select_fusion
  25.7 0.0 copy-start.4
  25.7 0.1 collective-permute-start.2
  25.8 2.6 %collective-permute-done.4.refs_3_ = bf16[656,1024]{1,0:T(8,128)(2,1)} collective-permute-done((bf16[656,1024]{1,0:T(8,128)(2,1)S(1)}, bf16[656,1024]{1,0:T(8,128)(2,1)}, u32[]{:S(2)}, u32[]{:S(2)}) %collective-permute-start.4) | collective-permute-done | bytes 1343520 | tf_op jit(solution)/shard_map/ppermute | solution.py:386
  28.3 9.5 %shard_map.101 = (f32[16,1,640]{2,1,0:T(1,128)S(1)}, bf16[4,1024,640]{2,1,0:T(8,128)(2,1)S(1)}, f32[4,8,640]{2,1,0:T(8,128)S(1)}) custom-call(s32[16,4]{1,0:T(8,128)S(1)} %copy-done.1, s32[16,15]{1,0:T(8,128)S(1)} %copy-done.2, bf16[656,1024]{1,0:T(8,128)(2,1)S(1)} %copy-done, bf16[656,1024]{1,0:T(8,128)(2,1)S(1)} %collective-permute-done.1.refs_1_, ...), custom_call_target="tpu_custom_call" | custom-call | tf_op jit(solution)/shard_map/pallas_call | solution.py:367
  37.9 1.6 %collective-permute-done.3.far = bf16[672,1024]{1,0:T(8,128)(2,1)} collective-permute-done((bf16[672,1024]{1,0:T(8,128)(2,1)}, bf16[672,1024]{1,0:T(8,128)(2,1)}, u32[]{:S(2)}, u32[]{:S(2)}) %collective-permute-start.3) | collective-permute-done | bytes 1376288 | tf_op jit(solution)/shard_map/ppermute | solution.py:383
  39.5 0.7 %collective-permute-start.5 = (bf16[672,1024]{1,0:T(8,128)(2,1)}, bf16[672,1024]{1,0:T(8,128)(2,1)S(1)}, u32[]{:S(2)}, u32[]{:S(2)}) collective-permute-start(bf16[672,1024]{1,0:T(8,128)(2,1)} %collective-permute-done.3.far), channel_id=1, source_target_pairs={{12,13},{13,12},{14,15},{15,14},{28,29},{29,28},{30,31},{31,30},{4... | collective-permute-start | bytes 4128776 | tf_op jit(solution)/shard_map/ppermute | solution.py:399
  40.3 4.7 %shard_map.102 = (f32[16,1,640]{2,1,0:T(1,128)S(1)}, bf16[1024,640]{1,0:T(8,128)(2,1)S(1)}, f32[8,640]{1,0:T(8,128)S(1)}) custom-call(s32[16,14]{1,0:T(8,128)S(1)} %copy-done.6, s32[16,4]{1,0:T(8,128)S(1)} %copy-done.4, bf16[672,1024]{1,0:T(8,128)(2,1)} %collective-permute-done.3.far, bf16[4,1024,640]{2,1,0:T(8,128)(2,1)S(1)} %get-tuple-element.26.turned, ...), custom_call_target="tpu_custom_call" | custom-call | flops 20000000000 | tf_op jit(solution)/shard_map/pallas_call | solution.py:367
  45.0 3.5 %shard_map.103.out = f32[16,1,640]{2,1,0:T(1,128)S(1)} custom-call(s32[16,14]{1,0:T(8,128)S(1)} %copy-done.5, s32[16,4]{1,0:T(8,128)S(1)} %copy-done.4, bf16[656,1024]{1,0:T(8,128)(2,1)S(1)} %collective-permute-done.2.block, bf16[672,1024]{1,0:T(8,128)(2,1)S(1)} %collective-permute-done.5.far_other, bf16[4,1024,640]{2,1,0:T(8,128)(2,1)S(1)} %get-tuple-element.26.turned, ...), custom_call_target="tpu_custom_call" | custom-call | tf_op jit(solution)/shard_map/pallas_call | solution.py:367
  48.6 1.5 %collective-permute-start.6 = (f32[16,1,640]{2,1,0:T(1,128)S(1)}, f32[16,1,640]{2,1,0:T(1,128)S(1)}, u32[]{:S(2)}, u32[]{:S(2)}) collective-permute-start(f32[16,1,640]{2,1,0:T(1,128)S(1)} %shard_map.103.out), channel_id=1, source_target_pairs={{0,1},{1,0},{2,3},{3,2},{4,5},{5,4},{6,7},{7,6},{8,9},{9,8},{10,11... | collective-permute-start | bytes 122888 | tf_op jit(solution)/shard_map/ppermute | solution.py:409
  50.0 0.9 %collective-permute-done.6.other = f32[16,1,640]{2,1,0:T(1,128)S(1)} collective-permute-done((f32[16,1,640]{2,1,0:T(1,128)S(1)}, f32[16,1,640]{2,1,0:T(1,128)S(1)}, u32[]{:S(2)}, u32[]{:S(2)}) %collective-permute-start.6) | collective-permute-done | bytes 40992 | tf_op jit(solution)/shard_map/ppermute | solution.py:409
  50.9 0.7 %shard_map.104 = (f32[2,1,640]{2,1,0:T(1,128)S(1)}, f32[2,1,640]{2,1,0:T(1,128)S(1)}, f32[2,1,640]{2,1,0:T(1,128)S(1)}) custom-call(s32[16,2]{1,0:T(8,128)S(1)} %copy-done.3, f32[16,1,640]{2,1,0:T(1,128)S(1)} %shard_map.103.out, f32[16,1,640]{2,1,0:T(1,128)S(1)} %collective-permute-done.6.other), custom_call_target="tpu_custom_call" | custom-call | tf_op jit(solution)/shard_map/pallas_call | solution.py:367
  51.6 0.5 collective-permute-start.7
  52.1 1.4 %collective-permute-start.8 = (f32[2,1,640]{2,1,0:T(1,128)S(1)}, f32[2,1,640]{2,1,0:T(1,128)S(1)}, u32[]{:S(2)}, u32[]{:S(2)}) collective-permute-start(f32[2,1,640]{2,1,0:T(1,128)S(1)} %get-tuple-element.36), channel_id=1, source_target_pairs={{0,6},{2,4},{4,12},{6,14},{8,0},{10,2},{12,8},{14,10},{1,5},{3,7},... | collective-permute-start | bytes 15368 | tf_op jit(solution)/shard_map/ppermute | solution.py:410
  53.5 0.7 %collective-permute-done.7.refs_1_ = f32[2,1,640]{2,1,0:T(1,128)S(1)} collective-permute-done((f32[2,1,640]{2,1,0:T(1,128)S(1)}, f32[2,1,640]{2,1,0:T(1,128)S(1)}, u32[]{:S(2)}, u32[]{:S(2)}) %collective-permute-start.7) | collective-permute-done | bytes 5152 | tf_op jit(solution)/shard_map/ppermute | solution.py:410
  54.2 1.6 %collective-permute-done.8.refs_2_ = f32[2,1,640]{2,1,0:T(1,128)S(1)} collective-permute-done((f32[2,1,640]{2,1,0:T(1,128)S(1)}, f32[2,1,640]{2,1,0:T(1,128)S(1)}, u32[]{:S(2)}, u32[]{:S(2)}) %collective-permute-start.8) | collective-permute-done | bytes 5152 | tf_op jit(solution)/shard_map/ppermute | solution.py:410
  55.8 5.3 %collective-permute-start.9 = (f32[1,640]{1,0:T(1,128)S(1)}, f32[1,640]{1,0:T(1,128)S(1)}, u32[]{:S(2)}, u32[]{:S(2)}) collective-permute-start(f32[1,640]{1,0:T(1,128)S(1)} %get-tuple-element.38), channel_id=1, source_target_pairs={{0,1},{1,0},{2,3},{3,2},{4,5},{5,4},{6,7},{7,6},{8,9},{9,8},{10,11... | collective-permute-start | bytes 7688 | tf_op jit(solution)/shard_map/ppermute | solution.py:412
  61.0 0.8 %collective-permute-done.9 = f32[1,640]{1,0:T(1,128)S(1)} collective-permute-done((f32[1,640]{1,0:T(1,128)S(1)}, f32[1,640]{1,0:T(1,128)S(1)}, u32[]{:S(2)}, u32[]{:S(2)}) %collective-permute-start.9) | collective-permute-done | bytes 2592 | tf_op jit(solution)/shard_map/ppermute | solution.py:412
  61.8 0.6 maximum_reduce_fusion
  (18 shorter events, 0.1 us)
Async XLA Ops:
  2.8 18.9 %collective-permute-start = (bf16[656,1024]{1,0:T(8,128)(2,1)}, bf16[656,1024]{1,0:T(8,128)(2,1)S(1)}, u32[]{:S(2)}, u32[]{:S(2)}) collective-permute-start(bf16[656,1024]{1,0:T(8,128)(2,1)} %get-tuple-element.22.refs_0_), channel_id=1, source_target_pairs={{0,2},{2,4},{4,6},{6,0},{8,10},{10,12},{12,14},{14,8},{1,7},{3,1},... | collective-permute-start | bytes 4030472 | tf_op jit(solution)/shard_map/ppermute | solution.py:382
  6.4 19.1 %collective-permute-start.1 = (bf16[656,1024]{1,0:T(8,128)(2,1)}, bf16[656,1024]{1,0:T(8,128)(2,1)S(1)}, u32[]{:S(2)}, u32[]{:S(2)}) collective-permute-start(bf16[656,1024]{1,0:T(8,128)(2,1)} %get-tuple-element.22.refs_0_), channel_id=1, source_target_pairs={{0,1},{1,0},{2,3},{3,2},{4,5},{5,4},{6,7},{7,6},{8,9},{9,8},{10,11... | collective-permute-start | bytes 4030472 | tf_op jit(solution)/shard_map/ppermute | solution.py:384
  6.4 33.1 %collective-permute-start.3 = (bf16[672,1024]{1,0:T(8,128)(2,1)}, bf16[672,1024]{1,0:T(8,128)(2,1)}, u32[]{:S(2)}, u32[]{:S(2)}) collective-permute-start(bf16[672,1024]{1,0:T(8,128)(2,1)} %get-tuple-element.23), channel_id=1, source_target_pairs={{0,8},{1,9},{2,10},{3,11},{4,12},{5,13},{6,14},{7,15},{8,0},{9,1},... | collective-permute-start | bytes 4128776 | tf_op jit(solution)/shard_map/ppermute | solution.py:383
  21.7 6.7 %collective-permute-start.4 = (bf16[656,1024]{1,0:T(8,128)(2,1)S(1)}, bf16[656,1024]{1,0:T(8,128)(2,1)}, u32[]{:S(2)}, u32[]{:S(2)}) collective-permute-start(bf16[656,1024]{1,0:T(8,128)(2,1)S(1)} %collective-permute-done.refs_2_), channel_id=1, source_target_pairs={{0,1},{1,0},{2,3},{3,2},{4,5},{5,4},{6,7},{7,6},{8,9},{9,8},{10,11... | collective-permute-start | bytes 4030472 | tf_op jit(solution)/shard_map/ppermute | solution.py:386
  25.5 2.8 %copy-start = (bf16[656,1024]{1,0:T(8,128)(2,1)S(1)}, bf16[656,1024]{1,0:T(8,128)(2,1)}, u32[]{:S(2)}) copy-start(bf16[656,1024]{1,0:T(8,128)(2,1)} %get-tuple-element.22.refs_0_) | copy-start | bytes 4030468
  25.5 2.8 %copy-start.1 = (s32[16,4]{1,0:T(8,128)S(1)}, s32[16,4]{1,0:T(8,128)}, u32[]{:S(2)}) copy-start(s32[16,4]{1,0:T(8,128)} %constant.22.clone.use) | copy-start | bytes 772
  25.5 2.8 %copy-start.2 = (s32[16,15]{1,0:T(8,128)S(1)}, s32[16,15]{1,0:T(8,128)}, u32[]{:S(2)}) copy-start(s32[16,15]{1,0:T(8,128)} %constant.23.clone.pairs) | copy-start | bytes 2884
  25.7 14.6 %copy-start.4 = (s32[16,4]{1,0:T(8,128)S(1)}, s32[16,4]{1,0:T(8,128)}, u32[]{:S(2)}) copy-start(s32[16,4]{1,0:T(8,128)} %constant.25.clone.meets) | copy-start | bytes 772
  25.7 14.6 %copy-start.6 = (s32[16,14]{1,0:T(8,128)S(1)}, s32[16,14]{1,0:T(8,128)}, u32[]{:S(2)}) copy-start(s32[16,14]{1,0:T(8,128)} %constant.24.clone.early) | copy-start | bytes 2692
  25.7 19.3 %collective-permute-start.2 = (bf16[656,1024]{1,0:T(8,128)(2,1)S(1)}, bf16[656,1024]{1,0:T(8,128)(2,1)S(1)}, u32[]{:S(2)}, u32[]{:S(2)}) collective-permute-start(bf16[656,1024]{1,0:T(8,128)(2,1)S(1)} %broadcast_select_fusion), channel_id=1, source_target_pairs={{0,2},{2,4},{4,6},{6,0},{8,10},{10,12},{12,14},{14,8},{1,7},{3,1},... | collective-permute-start | bytes 4030472 | tf_op jit(solution)/shard_map/ppermute | solution.py:385
  39.5 5.5 %collective-permute-start.5 = (bf16[672,1024]{1,0:T(8,128)(2,1)}, bf16[672,1024]{1,0:T(8,128)(2,1)S(1)}, u32[]{:S(2)}, u32[]{:S(2)}) collective-permute-start(bf16[672,1024]{1,0:T(8,128)(2,1)} %collective-permute-done.3.far), channel_id=1, source_target_pairs={{12,13},{13,12},{14,15},{15,14},{28,29},{29,28},{30,31},{31,30},{4... | collective-permute-start | bytes 4128776 | tf_op jit(solution)/shard_map/ppermute | solution.py:399
  40.3 4.8 %copy-start.5 = (s32[16,14]{1,0:T(8,128)S(1)}, s32[16,14]{1,0:T(8,128)}, u32[]{:S(2)}) copy-start(s32[16,14]{1,0:T(8,128)} %constant.26.clone.early) | copy-start | bytes 2692
  45.0 5.9 %copy-start.3 = (s32[16,2]{1,0:T(8,128)S(1)}, s32[16,2]{1,0:T(8,128)}, u32[]{:S(2)}) copy-start(s32[16,2]{1,0:T(8,128)} %constant.27.clone.targets) | copy-start | bytes 388
  48.6 2.3 %collective-permute-start.6 = (f32[16,1,640]{2,1,0:T(1,128)S(1)}, f32[16,1,640]{2,1,0:T(1,128)S(1)}, u32[]{:S(2)}, u32[]{:S(2)}) collective-permute-start(f32[16,1,640]{2,1,0:T(1,128)S(1)} %shard_map.103.out), channel_id=1, source_target_pairs={{0,1},{1,0},{2,3},{3,2},{4,5},{5,4},{6,7},{7,6},{8,9},{9,8},{10,11... | collective-permute-start | bytes 122888 | tf_op jit(solution)/shard_map/ppermute | solution.py:409
  51.6 2.5 %collective-permute-start.7 = (f32[2,1,640]{2,1,0:T(1,128)S(1)}, f32[2,1,640]{2,1,0:T(1,128)S(1)}, u32[]{:S(2)}, u32[]{:S(2)}) collective-permute-start(f32[2,1,640]{2,1,0:T(1,128)S(1)} %get-tuple-element.35), channel_id=1, source_target_pairs={{0,8},{2,10},{4,2},{6,0},{8,12},{10,14},{12,4},{14,6},{1,3},{3,1},... | collective-permute-start | bytes 15368 | tf_op jit(solution)/shard_map/ppermute | solution.py:410
  52.1 3.7 %collective-permute-start.8 = (f32[2,1,640]{2,1,0:T(1,128)S(1)}, f32[2,1,640]{2,1,0:T(1,128)S(1)}, u32[]{:S(2)}, u32[]{:S(2)}) collective-permute-start(f32[2,1,640]{2,1,0:T(1,128)S(1)} %get-tuple-element.36), channel_id=1, source_target_pairs={{0,6},{2,4},{4,12},{6,14},{8,0},{10,2},{12,8},{14,10},{1,5},{3,7},... | collective-permute-start | bytes 15368 | tf_op jit(solution)/shard_map/ppermute | solution.py:410
  55.8 6.1 %collective-permute-start.9 = (f32[1,640]{1,0:T(1,128)S(1)}, f32[1,640]{1,0:T(1,128)S(1)}, u32[]{:S(2)}, u32[]{:S(2)}) collective-permute-start(f32[1,640]{1,0:T(1,128)S(1)} %get-tuple-element.38), channel_id=1, source_target_pairs={{0,1},{1,0},{2,3},{3,2},{4,5},{5,4},{6,7},{7,6},{8,9},{9,8},{10,11... | collective-permute-start | bytes 7688 | tf_op jit(solution)/shard_map/ppermute | solution.py:412
